TPU v7x, 32 devices: a whole 2x2x4 slice. The times are simulated.
32 devices in a mesh: blk: 8 (over y, x, core), grp: 4 (over z).
Axes of the slice: x: 2, y: 2, z: 4, core: 2. Of those that a mesh axis runs over, the one named last changes fastest.
Arguments:
- amplitudes: bfloat16 [1024, 8, 4, 128], P('blk'), may hold values from -6 to 6
- integrals: bfloat16 [256, 1024, 128], P('grp', 'blk'), may hold values from -0.15625 to 0.15625
- virt_energy: float32 [1024], replicated, may hold values from 0.5 to 4
- pair_energy: float32 [8], replicated, may hold values from -3 to -0.5
- offsets: int32 [8, 4], replicated, may hold values from 0 to 7, as said below
Outputs:
- ladder: float32 [1024, 8, 4, 128], P(('blk', 'grp'))
- new_amplitudes: float32 [1024, 8, 4, 128], P(('blk', 'grp'))
Inputs may be any that keep to these rules, and one draw needn't show every extreme that they name: The 4 offsets of one row tile are different; the first 3 are at most 2, the last is larger than 2.
All inputs are finite; a program needn't handle non-finite values.
Results may differ from a plain program's by a relative error of at most 0.0029.
Values may be sent and summed in bfloat16 or wider, within the bound.
A program may use at most 64 MiB of HBM per device.

v0:
```python
import jax
import jax.numpy as jnp
from jax import lax
from jax.sharding import PartitionSpec as P


def local(amplitudes, integrals, virt_energy, pair_energy, offsets):
    tiles = lax.axis_size("blk")
    tile_index = lax.axis_index("blk")
    group_index = lax.axis_index("grp")
    slab_width = integrals.shape[2]
    aux_local = integrals.shape[0]
    pair_count = amplitudes.shape[1]
    slot_count = amplitudes.shape[2]
    own_offsets = lax.dynamic_slice_in_dim(offsets, tile_index, 1, 0)[0]
    cols = (tile_index - own_offsets) % tiles
    piece = lax.all_gather(integrals, "blk", axis=1, tiled=True)
    count = piece.shape[1] // slab_width
    tile_ids = jnp.arange(count, dtype=jnp.int32)
    onehot = (cols[:, None] == tile_ids[None, :]).astype(jnp.bfloat16)
    pieces = piece.reshape(aux_local, count, slab_width, slab_width)
    chosen = jnp.einsum("sj,qjbd->qsbd", onehot, pieces, preferred_element_type=jnp.float32)
    col_blocks = chosen.astype(jnp.bfloat16)
    flattened_rows = amplitudes.reshape(slab_width, pair_count * slot_count * slab_width)
    rows_per_device = slab_width // lax.axis_size("grp")

    def add_aux(aux, total):
        half_split = jnp.dot(
            integrals[aux], flattened_rows, preferred_element_type=jnp.float32
        ).astype(jnp.bfloat16)
        half_split = half_split.reshape(
            rows_per_device * lax.axis_size("grp"), pair_count, slot_count, slab_width
        )
        return total + jnp.einsum(
            "apsd,sbd->apsb", half_split, col_blocks[aux], preferred_element_type=jnp.float32
        )

    total_start_offset = jnp.zeros(
        (rows_per_device * lax.axis_size("grp"), pair_count, slot_count, slab_width), jnp.float32
    )
    ladder = lax.psum_scatter(
        lax.fori_loop(0, aux_local, add_aux, total_start_offset),
        "grp",
        scatter_dimension=0,
        tiled=True,
    )
    first_row = group_index * rows_per_device
    old_rows = lax.dynamic_slice_in_dim(amplitudes, first_row, rows_per_device, 0).astype(
        jnp.float32
    )
    row_energy = lax.dynamic_slice_in_dim(
        virt_energy, tile_index * slab_width + first_row, rows_per_device, 0
    )
    table = virt_energy.reshape(tiles, slab_width)
    selector = (cols[:, None] == jnp.arange(tiles, dtype=jnp.int32)[None, :]).astype(jnp.float32)
    col_energy = jnp.dot(selector, table, precision=lax.Precision.HIGHEST)
    denom = (
        row_energy[:, None, None, None]
        + col_energy[None, None, :, :]
        - pair_energy[None, :, None, None]
    )
    new_amplitudes = old_rows - ladder / denom
    return (ladder, new_amplitudes)


def solution(mesh):
    placed = (P("blk", None, None, None), P("grp", "blk", None), P(), P(), P())
    return jax.shard_map(
        local,
        mesh=mesh,
        in_specs=placed,
        out_specs=(P(("blk", "grp"), None, None, None), P(("blk", "grp"), None, None, None)),
        check_vma=False,
    )
```

profile of v0, /device:TPU:0, one launch (start us, length us, event | category | flops | bytes accessed | tf_op | source)
XLA Modules:
  0.0 609.3 jit_solution(869763255633171995)
XLA Ops:
  9.4 93.1 %all-gather.2.cloned.1.call-done = bf16[64,1024,128]{2,1,0:T(8,128)(2,1)} async-done(((bf16[64,128,128]{2,1,0:T(8,128)(2,1)}), bf16[64,1024,128]{2,1,0:T(8,128)(2,1)}) %all-gather.2.cloned.1.call-update) | async-done | bytes 16777232 | tf_op jit(solution)/shard_map/all_gather | solution.py:17
  102.5 18.0 %convert_bitcast_fusion = bf16[64,4,128,128]{3,1,2,0:T(4,128)(2,1)} fusion(bf16[64,8,128,128]{3,2,1,0:T(8,128)(2,1)} %bitcast.31, s32[4]{0:T(128)S(1)} %and_select_fusion), kind=kOutput, calls=%fused_computation.10 | convolution fusion | flops 71303200 | bytes 25165840 | tf_op jit(solution)/shard_map/sj,qjbd->qsbd/dot_general | solution.py:22
  120.5 431.5 %while.14 = (s32[]{:T(128)}, f32[128,8,4,128]{0,3,1,2:T(8,128)}, bf16[64,4,128,128]{3,1,2,0:T(4,128)(2,1)}, bf16[64,128,128]{2,1,0:T(8,128)(2,1)}, bf16[128,4096]{1,0:T(8,128)(2,1)S(1)}, /*index=5*/s32[]{:T(128)}, s32[]{:T(128)}) while((s32[]{:T(128)}, f32[128,8,4,128]{0,3,1,2:T(8,128)}, bf16[64,4,128,128]{3,1,2,0:T(4,128)(2,1)}, ...), condition=%wide.region_1.2_spmd.clone, body=%wide.region_0.1_spmd.clone.sunk | while | flops 270008320 | bytes 9863271 | solution.py:42
  128.6 3.9 bitcast_add_fusion.2
  135.4 3.8 bitcast_add_fusion.2
  148.9 3.9 bitcast_add_fusion.2
  155.7 3.8 bitcast_add_fusion.2
  162.5 3.8 bitcast_add_fusion.2
  169.2 3.9 bitcast_add_fusion.2
  176.0 3.8 bitcast_add_fusion.2
  182.8 3.8 bitcast_add_fusion.2
  189.5 3.9 bitcast_add_fusion.2
  196.3 3.8 bitcast_add_fusion.2
  209.8 3.9 bitcast_add_fusion.2
  216.6 3.8 bitcast_add_fusion.2
  230.1 3.9 bitcast_add_fusion.2
  236.9 3.8 bitcast_add_fusion.2
  250.5 3.9 bitcast_add_fusion.2
  257.2 3.8 bitcast_add_fusion.2
  270.8 3.9 bitcast_add_fusion.2
  277.5 3.8 bitcast_add_fusion.2
  291.1 3.9 bitcast_add_fusion.2
  297.8 3.8 bitcast_add_fusion.2
  311.4 3.9 bitcast_add_fusion.2
  318.1 3.8 bitcast_add_fusion.2
  331.7 3.9 bitcast_add_fusion.2
  338.4 3.8 bitcast_add_fusion.2
  352.0 3.9 bitcast_add_fusion.2
  358.7 3.8 bitcast_add_fusion.2
  372.3 3.9 bitcast_add_fusion.2
  379.0 3.8 bitcast_add_fusion.2
  392.6 3.9 bitcast_add_fusion.2
  399.3 3.8 bitcast_add_fusion.2
  412.9 3.9 bitcast_add_fusion.2
  419.6 3.8 bitcast_add_fusion.2
  433.2 3.9 bitcast_add_fusion.2
  439.9 3.8 bitcast_add_fusion.2
  453.5 3.9 bitcast_add_fusion.2
  460.3 3.8 bitcast_add_fusion.2
  473.8 3.9 bitcast_add_fusion.2
  480.6 3.8 bitcast_add_fusion.2
  494.1 3.9 bitcast_add_fusion.2
  500.9 3.8 bitcast_add_fusion.2
  514.4 3.9 bitcast_add_fusion.2
  521.2 3.8 bitcast_add_fusion.2
  534.7 3.9 bitcast_add_fusion.2
  541.5 3.8 bitcast_add_fusion.2
  557.3 42.0 %reduce-scatter.2.cloned.1.call-done = f32[32,8,4,128]{3,1,2,0:T(8,128)} async-done(((f32[128,8,4,128]{3,1,2,0:T(8,128)}), f32[32,8,4,128]{3,1,2,0:T(8,128)}) %reduce-scatter.2.cloned.1.call-update) | async-done | bytes 524304 | tf_op jit(solution)/shard_map/reduce_scatter | solution.py:41
  (238 shorter events, 271.4 us)
Async XLA Ops:
  7.2 1.2 copy-start.1
  7.2 2.0 copy-start.2
  7.2 95.3 %all-gather.2.cloned.1.call-start = ((), (), s32[]{:S(2)}) async-start(), calls=%async_computation.1 | async-start | bytes 18874368 | tf_op jit(solution)/shard_map/all_gather | solution.py:17
  7.9 591.4 %reduce-scatter.2.cloned.1.call-start = ((), (), s32[]{:S(2)}) async-start(), calls=%async_computation.2 | async-start | bytes 2621440 | tf_op jit(solution)/shard_map/reduce_scatter | solution.py:41
  555.2 0.7 copy-start.4
  555.2 44.1 %copy-start.3 = (f32[8]{0:T(128)S(1)}, f32[8]{0:T(128)}, u32[]{:S(2)}) copy-start(f32[8]{0:T(128)} %param.10) | copy-start | bytes 100
  599.3 2.2 copy-start
Sparse Core Ops, SparseCore 0:
  9.9 92.5 all-gather.1
  555.4 43.8 reduce-scatter.1
where the time goes:
time: 617 us; the launch traced here: 609 us
  matrix products  339 us (55%)
  waiting for transfers between devices  136 us (22%)
  local copies, waits for them, and re-layouts  118 us (19%)
  between operations  14.1 us (2%)
    dot_general x64, matrix products, add_aux(): jnp.einsum('apsd,sbd->apsb', half_split, col_blocks[aux], preferred_eleme...  245 us
    all_gather x1, waiting for transfers between devices, local(): piece = lax.all_gather(integrals, 'blk', axis=1, tiled=True)  93.1 us
    dot_general x64, matrix products, add_aux(): jnp.dot(integrals[aux], flattened_rows, preferred_element_type=jnp.float32)  75.7 us
    dynamic_slice x64, local copies, waits for them, and re-layouts, add_aux(): col_blocks[aux]  60.8 us
    reshape x64, local copies, waits for them, and re-layouts, add_aux(): half_split.reshape(rows_per_device * lax.axis_size('grp'), pair_count, sl...  49 us
    reduce_scatter x1, waiting for transfers between devices, local(): lax.psum_scatter(lax.fori_loop(0, aux_local, add_aux, total_start_offset)...  42 us
    dot_general x1, matrix products, local(): jnp.einsum('sj,qjbd->qsbd', onehot, pieces, preferred_element_type=jnp.fl...  18 us
  transfers between devices with their start and end apart: 2, of which 2 were waited for; matrix products, arithmetic and copies ran while one was open for 0% of the time, Pallas kernels for 0%

commit v1 on v0

v1 whole, which is shorter than its diff:
```python
import functools

import jax
import jax.numpy as jnp
from jax import lax
from jax.experimental import pallas as pl
from jax.experimental.pallas import tpu as pltpu
from jax.sharding import PartitionSpec as P

MESH = pl.DeviceIdType.MESH
GROUP = 4


def grid_of(chips):
    rows = max(d for d in range(1, chips + 1) if chips % d == 0 and d * d <= chips)
    return rows, chips // rows


def kernel(tiles, groups, chunks, sel_ref, amp_ref, int_ref, out_ref, *scratch):
    gath = scratch[:chunks]
    acc, out_buf, in_buf, send_sem, recv_sem, red_send, red_recv = scratch[chunks:]
    rows_of, cols_of = grid_of(tiles // 2)
    slots = amp_ref.shape[0]
    aux, width = int_ref.shape[0], int_ref.shape[1]
    pairs = amp_ref.shape[2] // width
    share = width // groups
    depth = aux // chunks
    part = depth // 2

    me = lax.axis_index("blk")
    grp = lax.axis_index("grp")
    core = lax.rem(me, 2)
    chip = me // 2
    hi = chip // cols_of
    lo = lax.rem(chip, cols_of)

    def tile_at(dy, dx, other=False):
        y = lax.rem(hi + dy, rows_of)
        x = lax.rem(lo + dx, cols_of)
        return (y * cols_of + x) * 2 + ((1 - core) if other else core)

    sibling = tile_at(0, 0, True)
    steps_y, steps_x = range(1, rows_of), range(1, cols_of)
    friends = [sibling] + [tile_at(0, d) for d in steps_x] + [tile_at(d, 0) for d in steps_y]

    barrier = pltpu.get_barrier_semaphore()
    for friend in friends:
        pl.semaphore_signal(barrier, inc=1, device_id={"blk": friend}, device_id_type=MESH)
    for d in range(1, groups):
        pl.semaphore_signal(
            barrier, inc=1, device_id={"grp": lax.rem(grp + d, groups)}, device_id_type=MESH
        )
    pl.semaphore_wait(barrier, len(friends) + groups - 1)

    sent = []

    def piece(c, tile, h):
        return gath[c].at[tile, pl.ds(h * part, part)]

    def send(src, c, tile, h, to):
        copy = pltpu.make_async_remote_copy(
            src_ref=src,
            dst_ref=piece(c, tile, h),
            send_sem=send_sem.at[len(sent)],
            recv_sem=recv_sem.at[tile, c, h],
            device_id={"blk": to},
            device_id_type=MESH,
        )
        copy.start()
        sent.append(copy)

    def arrived(c, tile, h):
        pltpu.make_async_remote_copy(
            src_ref=piece(c, tile, h),
            dst_ref=piece(c, tile, h),
            send_sem=send_sem.at[0],
            recv_sem=recv_sem.at[tile, c, h],
            device_id={"blk": sibling},
            device_id_type=MESH,
        ).wait_recv()

    def send_own(c):
        src = [int_ref.at[pl.ds(c * depth + h * part, part)] for h in (0, 1)]
        for h in (0, 1):
            for d in steps_x:
                send(src[h], c, me, h, tile_at(0, d))
            for d in steps_y:
                send(src[1 - h], c, me, 1 - h, tile_at(d, 0))
        for h in (0, 1):
            send(src[h], c, me, h, sibling)

    def relay(c):
        for first in (True, False):
            for d in steps_x:
                tile, h = tile_at(0, cols_of - d), 0 if first else 1
                arrived(c, tile, h)
                if first:
                    for e in steps_y:
                        send(piece(c, tile, h), c, tile, h, tile_at(e, 0))
                send(piece(c, tile, h), c, tile, h, sibling)
            for d in steps_y:
                tile, h = tile_at(rows_of - d, 0), 1 if first else 0
                arrived(c, tile, h)
                if first:
                    for e in steps_x:
                        send(piece(c, tile, h), c, tile, h, tile_at(0, e))
                send(piece(c, tile, h), c, tile, h, sibling)

    def hand_over(c):
        for h in (0, 1):
            for dy in steps_y:
                for dx in steps_x:
                    tile = tile_at(dy, dx)
                    arrived(c, tile, h)
                    send(piece(c, tile, h), c, tile, h, sibling)

    def from_sibling(c):
        for h in (0, 1):
            for dy in range(rows_of):
                for dx in range(cols_of):
                    arrived(c, tile_at(dy, dx, True), h)

    def work(c, order, slot, column):
        def body(i, _):
            first = i * GROUP
            own = int_ref[pl.ds(c * depth + first, GROUP)].reshape(GROUP * width, width)
            half = jnp.dot(own, amp_ref[slot], preferred_element_type=jnp.float32)
            half = half.astype(jnp.bfloat16)
            left = jnp.concatenate(
                [
                    jnp.concatenate(
                        [
                            half[g * width:(g + 1) * width, p * width:(p + 1) * width]
                            for g in range(GROUP)
                        ],
                        axis=1,
                    )
                    for p in range(pairs)
                ],
                axis=0,
            )
            block = column(first)
            right = jnp.concatenate([block[g] for g in range(GROUP)], axis=1)
            term = lax.dot_general(
                left, right, (((1,), (1,)), ((), ())), preferred_element_type=jnp.float32
            ).reshape(pairs, width, width)
            acc[order] += term
            return 0

        lax.fori_loop(0, depth // GROUP, body, 0)

    def reduce_copy(d, order):
        return pltpu.make_async_remote_copy(
            src_ref=out_buf.at[d - 1, order],
            dst_ref=in_buf.at[d - 1, order],
            send_sem=red_send.at[d - 1, order],
            recv_sem=red_recv.at[d - 1, order],
            device_id={"grp": lax.rem(grp + d, groups)},
            device_id_type=MESH,
        )

    def reduce_send(order):
        for d in range(1, groups):
            to = lax.rem(grp + d, groups)
            rows = acc[order, :, pl.ds(to * share, share), :].reshape(pairs * share, width)
            out_buf[d - 1, order] = rows.astype(jnp.bfloat16)
            reduce_copy(d, order).start()

    slot_of = [sel_ref[0, o] for o in range(slots)]
    far = sel_ref[1, slots - 1]

    send_own(0)
    if chunks > 1:
        send_own(1)
    acc[...] = jnp.zeros_like(acc)
    for c in range(chunks + 1):
        if c < chunks:
            work(c, 0, slot_of[0], lambda f: int_ref[pl.ds(c * depth + f, GROUP)])
            relay(c)
            if c + 2 < chunks:
                send_own(c + 2)
            if c == chunks - 1:
                reduce_send(0)
        if c > 0:
            b = c - 1
            hand_over(b)
            from_sibling(b)
            for o in range(1, slots - 1):
                near = lax.rem(me + tiles - o, tiles)
                work(b, o, slot_of[o], lambda f: gath[b][near, pl.ds(f, GROUP)])
                if b == chunks - 1:
                    reduce_send(o)
            work(b, slots - 1, slot_of[slots - 1], lambda f: gath[b][far, pl.ds(f, GROUP)])
    reduce_send(slots - 1)
    for copy in sent:
        copy.wait_send()
    for o in range(slots):
        for d in range(1, groups):
            reduce_copy(d, o).wait()
    for s in range(slots):
        o = sel_ref[2, s]
        total = acc[o, :, pl.ds(grp * share, share), :].reshape(pairs * share, width)
        for d in range(1, groups):
            total = total + in_buf[d - 1, o].astype(jnp.float32)
        out_ref[s] = total


def local(tiles, groups, amplitudes, integrals, virt_energy, pair_energy, offsets):
    tile_index = lax.axis_index("blk")
    group_index = lax.axis_index("grp")
    aux, width = integrals.shape[0], integrals.shape[2]
    pairs, slots = amplitudes.shape[1], amplitudes.shape[2]
    share = width // groups
    chunks = max(2, min(4, 32 // tiles))
    own_offsets = lax.dynamic_slice_in_dim(offsets, tile_index, 1, 0)[0]
    cols = (tile_index - own_offsets) % tiles
    ids = jnp.arange(slots, dtype=jnp.int32)
    place = jnp.where(ids == slots - 1, slots - 1, own_offsets)
    slot_of = jnp.sum(jnp.where(place[None, :] == ids[:, None], ids[None, :], 0), axis=1)
    select = jnp.stack([slot_of, jnp.broadcast_to(cols[slots - 1], (slots,)), place])
    select = select.astype(jnp.int32)
    by_slot = amplitudes.transpose(2, 0, 1, 3).reshape(slots, width, pairs * width)

    rows_of, cols_of = grid_of(tiles // 2)
    y, x = rows_of - 1, cols_of - 1
    n_sent = chunks * (2 * (1 + x + y) + 2 * x * y + 2 * (x + y + x * y))
    depth = aux // chunks
    summed = pl.pallas_call(
        functools.partial(kernel, tiles, groups, chunks),
        out_shape=jax.ShapeDtypeStruct((slots, pairs * share, width), jnp.float32),
        in_specs=[
            pl.BlockSpec(memory_space=pltpu.SMEM),
            pl.BlockSpec(memory_space=pltpu.VMEM),
            pl.BlockSpec(memory_space=pltpu.VMEM),
        ],
        out_specs=pl.BlockSpec(memory_space=pltpu.VMEM),
        scratch_shapes=[pltpu.VMEM((tiles, depth, width, width), jnp.bfloat16)] * chunks
        + [
            pltpu.VMEM((slots, pairs, width, width), jnp.float32),
            pltpu.VMEM((groups - 1, slots, pairs * share, width), jnp.bfloat16),
            pltpu.VMEM((groups - 1, slots, pairs * share, width), jnp.bfloat16),
            pltpu.SemaphoreType.DMA((n_sent,)),
            pltpu.SemaphoreType.DMA((tiles, chunks, 2)),
            pltpu.SemaphoreType.DMA((groups - 1, slots)),
            pltpu.SemaphoreType.DMA((groups - 1, slots)),
        ],
        compiler_params=pltpu.CompilerParams(
            collective_id=0, has_side_effects=True, vmem_limit_bytes=56 << 20
        ),
        cost_estimate=pl.CostEstimate(
            flops=4 * aux * slots * pairs * width**3,
            bytes_accessed=4 << 20,
            transcendentals=0,
        ),
    )(select, by_slot, integrals)
    ladder = summed.reshape(slots, pairs, share, width).transpose(2, 1, 0, 3)

    first_row = group_index * share
    old_rows = lax.dynamic_slice_in_dim(amplitudes, first_row, share, 0).astype(jnp.float32)
    row_energy = lax.dynamic_slice_in_dim(virt_energy, tile_index * width + first_row, share, 0)
    table = virt_energy.reshape(tiles, width)
    col_energy = jnp.stack(
        [lax.dynamic_index_in_dim(table, cols[s], 0, keepdims=False) for s in range(slots)]
    )
    denom = (
        row_energy[:, None, None, None]
        + col_energy[None, None, :, :]
        - pair_energy[None, :, None, None]
    )
    return ladder, old_rows - ladder / denom


def solution(mesh):
    placed = (P("blk", None, None, None), P("grp", "blk", None), P(), P(), P())
    return jax.shard_map(
        functools.partial(local, mesh.shape["blk"], mesh.shape["grp"]),
        mesh=mesh,
        in_specs=placed,
        out_specs=(P(("blk", "grp"), None, None, None), P(("blk", "grp"), None, None, None)),
        check_vma=False,
    )
```

time: 617 us -> 122 us (0.20); the launches traced: 609 us -> 122 us
  matrix products: 339 us -> 0 us
  waiting for transfers between devices: 136 us -> 0 us
  local copies, waits for them, and re-layouts: 118 us -> 5.73 us
  Pallas kernels: 0 us -> 104 us
    dot_general x130 -> x0, matrix products: 339 us -> none  [the longest x64 245 us: add_aux(): jnp.einsum('apsd,sbd->apsb', half_split, col_blocks[aux], preferred_eleme...]
    pallas_call x0 -> x1, Pallas kernels: none -> 104 us  [local(): pl.pallas_call(functools.partial(kernel, tiles, groups, chunks), out_shap...]
    all_gather x1 -> x0, waiting for transfers between devices: 93.1 us -> none  [local(): piece = lax.all_gather(integrals, 'blk', axis=1, tiled=True)]
    dynamic_slice x66 -> x3, local copies, waits for them, and re-layouts: 61.9 us -> 1.67 us  [the longest x1 0.84 us: local(): lax.dynamic_index_in_dim(table, cols[s], 0, keepdims=False)]
    reshape x65 -> x1, local copies, waits for them, and re-layouts: 49.8 us -> 1.26 us  [local(): amplitudes.transpose(2, 0, 1, 3).reshape(slots, width, pairs * width)]
    reduce_scatter x1 -> x0, waiting for transfers between devices: 42 us -> none  [local(): lax.psum_scatter(lax.fori_loop(0, aux_local, add_aux, total_start_offset)...]
  transfers between devices with their start and end apart: 2 -> 0, of which waited for: 2 -> 0; matrix products, arithmetic and copies ran while one was open for 0% -> 0% of each run, Pallas kernels for 0% -> 0%
where the time goes in v1:
time: 122 us
  Pallas kernels  104 us (85%)
  between operations  8.24 us (7%)
  local copies, waits for them, and re-layouts  5.73 us (5%)
  other arithmetic  3.5 us (3%)
    pallas_call x1, Pallas kernels, local(): pl.pallas_call(functools.partial(kernel, tiles, groups, chunks), out_shap...  104 us
    sub x1, other arithmetic, local(): return (ladder, old_rows - ladder / denom)  2.61 us

profile of v1, /device:TPU:0, one launch (start us, length us, event | category | flops | bytes accessed | tf_op | source)
XLA Modules:
  0.0 121.8 jit_solution(8060560027435859192)
XLA Ops:
  0.6 0.0 copy-start
  0.7 0.8 dynamic_slice.24
  1.4 0.0 copy-done
  1.4 0.1 constant_dynamic-slice_fusion.4
  1.5 0.1 copy.13
  1.6 0.1 select_reduce_fusion
  1.7 0.6 fusion.2
  9.9 0.7 pad.5.clone
  10.6 0.8 constant_dynamic-slice_fusion.3
  11.5 0.6 pad_add_fusion.sel_ref
  12.1 0.1 broadcast_add_fusion
  12.2 1.4 %copy.11 = bf16[4,128,8,128]{3,2,1,0:T(8,128)(2,1)S(1)} copy(bf16[4,128,8,128]{3,0,2,1:T(4,128)(2,1)} %bitcast.17) | data formatting | bytes 2097152 | tf_op jit(solution)/shard_map/transpose | solution.py:222
  13.6 1.3 %reshape.31.amp_ref = bf16[4,128,1024]{2,1,0:T(8,128)(2,1)} reshape(bf16[4,128,8,128]{3,2,1,0:T(8,128)(2,1)S(1)} %copy.11) | data formatting | bytes 2097152 | tf_op jit(solution)/shard_map/reshape | solution.py:222
  14.8 0.0 copy-start.1
  14.8 104.3 %shard_map.68 = f32[4,256,128]{2,1,0:T(8,128)} custom-call(s32[3,4]{1,0:T(4,128)} %pad_add_fusion.sel_ref, bf16[4,128,1024]{2,1,0:T(8,128)(2,1)} %reshape.31.amp_ref, bf16[64,128,128]{2,1,0:T(8,128)(2,1)} %int_ref.1), custom_call_target="tpu_custom_call" | custom-call | flops 17179869184 | bytes 4194304 | tf_op jit(solution)/shard_map/pallas_call | solution.py:228
  119.1 0.0 copy-done.1
  119.1 2.6 %divide_subtract_fusion = (f32[32,8,4,128]{3,2,1,0:T(4,128)}, f32[32,8,4,128]{3,2,1,0:T(4,128)}) fusion(f32[8]{0:T(128)S(1)} %copy-done.1, f32[32,4,128]{2,1,0:T(4,128)S(1)} %broadcast_add_fusion, bf16[128,8,4,128]{3,2,1,0:T(4,128)(2,1)} %param.5, s32[]{:T(128)S(6)} %select_n.42, f32[4,8,32,128]{3,2,1,0:T(8,128)} %bitcast.18), kind=kLoop, calls=%fused_computation.1 | loop fusion | flops 524288 | bytes 1900580 | tf_op jit(solution)/shard_map/sub | solution.py:270
  (3 shorter events, 0.0 us)
Async XLA Ops:
  0.6 0.8 copy-start
  14.8 104.3 %copy-start.1 = (f32[8]{0:T(128)S(1)}, f32[8]{0:T(128)}, u32[]{:S(2)}) copy-start(f32[8]{0:T(128)} %param.8) | copy-start | bytes 100
